TPU v7x, 32 devices: a whole 2x2x4 slice. The times are simulated.
32 devices in a mesh: parts: 2 (over y), tensor: 8 (over z, x), dp: 2 (over core).
Axes of the slice: x: 2, y: 2, z: 4, core: 2. Of those that a mesh axis runs over, the one named last changes fastest.
Arguments:
- cotangent: bfloat16 [8192, 2048], P('tensor', ('parts', 'dp')), parts along dimension 1, may hold values from -6 to 6
- layer_input: bfloat16 [8192, 2048], P('tensor', ('parts', 'dp')), parts along dimension 1, may hold values from -6 to 6
- gate_pre: bfloat16 [28672, 2048], P('tensor', ('parts', 'dp')), parts along dimension 1, may hold values from -6 to 6
- up_pre: bfloat16 [28672, 2048], P('tensor', ('parts', 'dp')), parts along dimension 1, may hold values from -6 to 6
- down_weight: bfloat16 [28672, 8192], P('tensor'), may hold values from -0.0625 to 0.0625
- proj_input: bfloat16 [8192, 64], P('tensor'), may hold values from -0.0625 to 0.0625
- proj_gate: bfloat16 [28672, 64], P('tensor'), may hold values from -0.03125 to 0.03125
- proj_up: bfloat16 [28672, 64], P('tensor'), may hold values from -0.03125 to 0.03125
- store_slot: int32 [16], P(('parts', 'dp')), parts along dimension 0, may hold values from 0 to 7, each once
- example_ids: int32 [16], P(('parts', 'dp')), parts along dimension 0, may hold values from 0 to 999999
- lengths: int32 [16], P(('parts', 'dp')), parts along dimension 0, may hold values from 1 to 128, 768 in all
Outputs:
- store_keys: bfloat16 [16, 8192], P(('parts', 'dp')), parts along dimension 0
- store_ids: int32 [16], P(('parts', 'dp')), parts along dimension 0
There are 2 independent parts, one for each index of `parts`. A program takes and returns all parts, laid end to end along the dimension named above; an argument that names none is the same for every part. Nothing has to cross between parts.
Inputs may be any that keep to these rules, and one draw needn't show every extreme that they name: `store_slot`: each of 0 to 7 appears exactly once.
All inputs are finite; a program needn't handle non-finite values. No bound on the sum of `lengths` on one device may be relied on, other than what follows from the above.
Results may differ from a plain program's by a relative error of at most 0.0052.
Values may be sent and summed in bfloat16 or wider, within the bound.
A program may use at most 192 MiB of HBM per device.

v0:
```python
import jax
import jax.numpy as jnp
from jax import lax
from jax.sharding import PartitionSpec as P


def silu_parts(gate_value):
    sigmoid_gate = jax.nn.sigmoid(gate_value)
    return (gate_value * sigmoid_gate, sigmoid_gate * (1.0 + gate_value * (1.0 - sigmoid_gate)))


def contract_first(left, right):
    return lax.dot_general(
        left, right, (((0,), (0,)), ((), ())), preferred_element_type=jnp.float32
    )


def per_device(
    cotangent,
    layer_input,
    gate_pre,
    up_pre,
    down_weight,
    proj_input,
    proj_gate,
    proj_up,
    store_slot,
    example_ids,
    lengths,
):
    tok_count = cotangent.shape[1]
    proj_rank = proj_gate.shape[1]
    seq_count = lengths.shape[0]
    seq_len = tok_count // seq_count
    hidden_grad = jnp.dot(
        down_weight,
        lax.all_gather(cotangent, "tensor", axis=0, tiled=True),
        preferred_element_type=jnp.float32,
    )
    input_partial = contract_first(proj_input, layer_input)
    gate_value = gate_pre.astype(jnp.float32)
    up_value = up_pre.astype(jnp.float32)
    activated, slope = silu_parts(gate_value)
    gate_grad = (hidden_grad * up_value * slope).astype(jnp.bfloat16)
    up_grad = (hidden_grad * activated).astype(jnp.bfloat16)
    gate_factor = contract_first(proj_gate, gate_grad)
    up_factor = contract_first(proj_up, up_grad)
    partial_rows = jnp.concatenate([gate_factor, up_factor, input_partial], axis=0)
    inverse_root = lax.rsqrt(lengths.astype(jnp.float32))
    summed = lax.psum(partial_rows, "tensor")
    input_factor = summed[2 * proj_rank :]
    position = jnp.arange(seq_len, dtype=jnp.int32)
    inside = jnp.where(position[None, :] < lengths[:, None], 1.0, 0.0).astype(jnp.float32)
    weight = inside * inverse_root[:, None]
    grads_three = summed[: 2 * proj_rank].reshape(2, proj_rank, seq_count, seq_len)
    inputs_three = input_factor.reshape(proj_rank, seq_count, seq_len)
    key_values = jnp.einsum(
        "gael,bel,el->egab", grads_three, inputs_three, weight, precision=lax.Precision.HIGHEST
    )
    key_values = key_values.reshape(seq_count, -1)
    key_rows = key_values.astype(jnp.bfloat16)
    dp_count = lax.axis_size("dp")
    slot_index = jnp.arange(dp_count * seq_count, dtype=jnp.int32)
    chosen = store_slot[None, :] == slot_index[:, None]
    outgoing = jnp.dot(
        chosen.astype(jnp.bfloat16), key_rows, preferred_element_type=jnp.float32
    ).astype(jnp.bfloat16)
    outgoing = outgoing.reshape(dp_count, seq_count, -1)
    outgoing_ids = jnp.sum(jnp.where(chosen, example_ids[None, :], 0), axis=1).reshape(
        dp_count, seq_count
    )
    arrived, arrived_ids = (
        lax.all_to_all(outgoing, "dp", split_axis=0, concat_axis=0, tiled=True),
        lax.all_to_all(outgoing_ids, "dp", split_axis=0, concat_axis=0, tiled=True),
    )
    store_keys = jnp.sum(arrived.astype(jnp.float32), axis=0).astype(jnp.bfloat16)
    store_ids = jnp.sum(arrived_ids, axis=0).astype(jnp.int32)
    return (store_keys, store_ids)


def solution(mesh):
    placed = (
        P("tensor", ("parts", "dp")),
        P("tensor", ("parts", "dp")),
        P("tensor", ("parts", "dp")),
        P("tensor", ("parts", "dp")),
        P("tensor", None),
        P("tensor", None),
        P("tensor", None),
        P("tensor", None),
        P(("parts", "dp")),
        P(("parts", "dp")),
        P(("parts", "dp")),
    )
    return jax.shard_map(
        per_device,
        mesh=mesh,
        in_specs=placed,
        out_specs=(P(("parts", "dp"), None), P(("parts", "dp"))),
        check_vma=False,
    )
```

profile of v0, /device:TPU:0, one launch (start us, length us, event | category | flops | bytes accessed | tf_op | source)
XLA Modules:
  0.0 267.1 jit_solution(7844852962875307444)
XLA Ops:
  7.2 0.0 copy-start
  7.2 0.0 all-gather.2.cloned.1.call-start
  7.2 0.7 all-gather.2.cloned.1.call-update
  7.9 0.0 all-reduce.2.cloned.1.call-start
  8.0 0.8 select_reduce_fusion
  8.7 0.1 all_to_all.10
  8.8 3.6 %all_to_all.14 = s32[2,1,4]{2,1,0:T(1,128)S(1)} all-to-all(s32[2,1,4]{2,1,0:T(1,128)S(1)} %bitcast.30), channel_id=1, replica_groups=mesh['parts'=2,'tensor'=8,'dp'=2] {'dp'}, dimensions={0} | all-to-all | bytes 64 | tf_op jit(solution)/shard_map/all_to_all | solution.py:74
  12.4 0.5 reduce_sum.32
  13.0 1.2 fusion.28
  14.2 0.0 copy-start.6
  14.2 123.6 %all-gather.2.cloned.1.call-done = bf16[8192,512]{1,0:T(8,128)(2,1)} async-done(((bf16[1024,512]{1,0:T(8,128)(2,1)}), bf16[8192,512]{1,0:T(8,128)(2,1)}) %all-gather.2.cloned.1.call-update) | async-done | bytes 8388624 | tf_op jit(solution)/shard_map/all_gather | solution.py:37
  137.8 38.8 %fusion.27 = f32[3584,512]{1,0:T(8,128)S(1)} fusion(bf16[3584,8192]{1,0:T(8,128)(2,1)} %param.15, bf16[8192,512]{1,0:T(8,128)(2,1)} %all-gather.2.cloned.1.call-done), kind=kOutput, calls=%fused_computation.33 | convolution fusion | flops 30064771072 | bytes 74448896 | tf_op jit(solution)/shard_map/dot_general | solution.py:35
  176.6 0.0 copy-start.5
  176.7 0.0 copy-start.7
  176.7 2.3 fusion.16
  179.0 0.0 copy-start.3
  179.0 0.0 copy-start.2
  179.0 0.0 copy-start.1
  179.0 3.3 %fusion.13 = f32[64,512]{1,0:T(8,128)S(1)} fusion(bf16[3584,64]{0,1:T(8,128)(2,1)S(1)} %copy-done.7, bf16[3584,512]{1,0:T(8,128)(2,1)S(1)} %copy-done.4, f32[3584,512]{1,0:T(8,128)S(1)} %fusion.27, bf16[3584,512]{1,0:T(8,128)(2,1)S(1)} %copy-done.5), kind=kOutput, calls=%fused_computation.16 | convolution fusion | flops 256901120 | bytes 15269888 | tf_op jit(solution)/shard_map/dot_general | solution.py:13
  182.3 0.8 pad_maximum_fusion
  183.1 0.0 all-reduce.2.cloned.1.call-update
  183.2 0.1 select_multiply_fusion
  183.2 69.6 %all-reduce.2.cloned.1.call-done = f32[192,512]{1,0:T(8,128)} async-done(((f32[192,512]{1,0:T(8,128)}), f32[192,512]{1,0:T(8,128)}) %all-reduce.2.cloned.1.call-update) | async-done | bytes 393232 | tf_op jit(solution)/shard_map/psum | solution.py:50
  252.8 1.0 slice.8
  253.8 0.1 reshape.23
  253.9 1.3 convolution_convert_fusion.1
  255.2 0.1 convert_element_type.33
  255.3 0.0 copy-done.2
  255.4 0.3 convolution_convert_fusion
  255.7 0.1 reshape.25
  255.7 3.8 %all_to_all.15 = bf16[2,4,8192]{2,1,0:T(4,128)(2,1)S(1)} all-to-all(bf16[2,4,8192]{2,1,0:T(4,128)(2,1)S(1)} %reshape.25), channel_id=1, replica_groups=mesh['parts'=2,'tensor'=8,'dp'=2] {'dp'}, dimensions={0} | all-to-all | bytes 262144 | tf_op jit(solution)/shard_map/all_to_all | solution.py:73
  259.6 0.7 reduce_sum.30
  (9 shorter events, 0.0 us)
Async XLA Ops:
  7.2 5.8 %copy-start = (bf16[1024,512]{1,0:T(8,128)(2,1)S(1)}, bf16[1024,512]{1,0:T(8,128)(2,1)}, u32[]{:S(2)}) copy-start(bf16[1024,512]{1,0:T(8,128)(2,1)} %param.12) | copy-start | bytes 3145732
  7.2 130.6 %all-gather.2.cloned.1.call-start = ((), (), s32[]{:S(2)}) async-start(), calls=%async_computation.2 | async-start | bytes 9437184 | tf_op jit(solution)/shard_map/all_gather | solution.py:37
  7.9 244.9 %all-reduce.2.cloned.1.call-start = ((), (), s32[]{:S(2)}) async-start(), calls=%async_computation.3 | async-start | bytes 786432 | tf_op jit(solution)/shard_map/psum | solution.py:50
  14.2 162.4 %copy-start.6 = (bf16[3584,64]{0,1:T(8,128)(2,1)S(1)}, bf16[3584,64]{0,1:T(8,128)(2,1)}, u32[]{:S(2)}) copy-start(bf16[3584,64]{0,1:T(8,128)(2,1)} %param.18) | copy-start | bytes 1376260
  137.8 38.8 %copy-start.4 = (bf16[3584,512]{1,0:T(8,128)(2,1)S(1)}, bf16[3584,512]{1,0:T(8,128)(2,1)}, u32[]{:S(2)}) copy-start(bf16[3584,512]{1,0:T(8,128)(2,1)} %param.13) | copy-start | bytes 11010052
  176.6 2.3 copy-start.5
  176.7 2.3 copy-start.7
  179.0 4.2 %copy-start.3 = (s32[4]{0:T(128)S(1)}, s32[4]{0:T(128)}, u32[]{:S(2)}) copy-start(s32[4]{0:T(128)} %param.21) | copy-start | bytes 52
  179.0 76.4 %copy-start.2 = (s32[4]{0:T(128)S(1)}, s32[4]{0:T(128)}, u32[]{:S(2)}) copy-start(s32[4]{0:T(128)} %param.19) | copy-start | bytes 52
  179.0 81.3 %copy-start.1 = (bf16[1024,512]{1,0:T(8,128)(2,1)S(1)}, bf16[1024,512]{1,0:T(8,128)(2,1)}, u32[]{:S(2)}) copy-start(bf16[1024,512]{1,0:T(8,128)(2,1)} %param.12) | copy-start | bytes 3145732
Sparse Core Ops, SparseCore 0:
  10.1 127.6 all-gather.1
  183.3 69.5 all-reduce.1
where the time goes:
time: 267 us
  waiting for transfers between devices  194 us (73%)
  matrix products  47.2 us (18%)
  between operations  14.2 us (5%)
  blocking collectives  7.48 us (3%)
  other arithmetic  2.85 us (1%)
    all_gather x1, waiting for transfers between devices, per_device(): lax.all_gather(cotangent, 'tensor', axis=0, tiled=True)  124 us
    psum x1, waiting for transfers between devices, per_device(): summed = lax.psum(partial_rows, 'tensor')  69.6 us
    dot_general x1, matrix products, per_device(): jnp.dot(down_weight, lax.all_gather(cotangent, 'tensor', axis=0, tiled=Tr...  38.8 us
    dot_general x3, matrix products, contract_first(): lax.dot_general(left, right, (((0,), (0,)), ((), ())), preferred_element_...  6.78 us
  transfers between devices with their start and end apart: 2, of which 2 were waited for; matrix products, arithmetic and copies ran while one was open for 1% of the time, Pallas kernels for 0%

commit v1 on v0

--- a/solution.py
+++ b/solution.py
@@ -1,7 +1,18 @@
+import functools
+
 import jax
 import jax.numpy as jnp
 from jax import lax
+from jax.experimental import pallas as pl
+from jax.experimental.pallas import tpu as pltpu
 from jax.sharding import PartitionSpec as P
+
+MESH = pl.DeviceIdType.MESH
+F32 = jnp.float32
+BF16 = jnp.bfloat16
+PIECES = 2
+W_SLOTS = 3
+ROWS = 512
 
 
 def silu_parts(gate_value):
@@ -15,7 +26,426 @@
     )
 
 
-def per_device(
+def contract_last(left, right):
+    return lax.dot_general(
+        left,
+        right,
+        (((1,), (1,)), ((), ())),
+        precision=lax.Precision.HIGHEST,
+        preferred_element_type=jnp.float32,
+    )
+
+
+def keys_kernel(
+    cot_ref,
+    w_ref,
+    gate_ref,
+    up_ref,
+    pg_ref,
+    pu_ref,
+    inp_ref,
+    mask_ref,
+    out_ref,
+    held,
+    wbuf,
+    acc,
+    gate_mul,
+    up_mul,
+    stage,
+    irecv,
+    iall,
+    frows,
+    frecv,
+    fall,
+    keys,
+    w_sem,
+    stage_sem,
+    recv_sem,
+    own_send,
+    x_send,
+    z_send,
+    isem_s,
+    isem_r,
+    jsem_s,
+    jsem_r,
+    fsem_s,
+    fsem_r,
+    ksem_s,
+    ksem_r,
+    dsem,
+):
+    feats, toks = cot_ref.shape
+    hidden = w_ref.shape[0]
+    depth = feats // PIECES
+    tiles = hidden // ROWS
+    me = lax.axis_index("tensor")
+    core = lax.axis_index("dp")
+    z, x = me // 2, me % 2
+    other = 1 - x
+    o1 = z - 1 + 2 * ((3 - z) // 3)
+    o3 = 3 * (1 - z // 2)
+    o2 = 6 - z - o1 - o3
+    across = {"tensor": z * 2 + other}
+    peer = {"dp": 1 - core}
+
+    order = [
+        me,
+        o1 * 2 + x,
+        z * 2 + other,
+        o2 * 2 + x,
+        o1 * 2 + other,
+        o3 * 2 + x,
+        o2 * 2 + other,
+        o3 * 2 + other,
+    ]
+    steps = [(shard, piece) for shard in range(8) for piece in range(PIECES)]
+
+    def w_copy(step):
+        index, piece = steps[step]
+        start = pl.multiple_of(order[index] * feats + piece * depth, depth)
+        return pltpu.make_async_copy(
+            w_ref.at[:, pl.ds(start, depth)], wbuf.at[step % W_SLOTS], w_sem.at[step % W_SLOTS]
+        )
+
+    for step in range(W_SLOTS):
+        w_copy(step).start()
+
+    barrier = pltpu.get_barrier_semaphore()
+    for shift in range(1, 8):
+        pl.semaphore_signal(
+            barrier, inc=1, device_id={"tensor": (me + shift) % 8}, device_id_type=MESH
+        )
+    pl.semaphore_signal(barrier, inc=1, device_id=peer, device_id_type=MESH)
+    pl.semaphore_wait(barrier, 8)
+
+    def remote(src, dst, send, recv, where):
+        return pltpu.make_async_remote_copy(
+            src_ref=src,
+            dst_ref=dst,
+            send_sem=send,
+            recv_sem=recv,
+            device_id=where,
+            device_id_type=MESH,
+        )
+
+    def own_copy(piece, way):
+        where = [
+            across,
+            {"tensor": jnp.minimum(me + 2, 6 + x)},
+            {"tensor": jnp.maximum(me - 2, x)},
+        ][way]
+        return remote(
+            cot_ref.at[pl.ds(piece * depth, depth)],
+            held.at[me, pl.ds(piece * depth, depth)],
+            own_send.at[way, piece],
+            recv_sem.at[me, piece],
+            where,
+        )
+
+    def x_copy(k, shard, piece):
+        block = held.at[shard, pl.ds(piece * depth, depth)]
+        return remote(block, block, x_send.at[k, piece], recv_sem.at[shard, piece], across)
+
+    def z_copy(k, shard, piece, way):
+        block = held.at[shard, pl.ds(piece * depth, depth)]
+        return remote(
+            block,
+            block,
+            z_send.at[k, piece],
+            recv_sem.at[shard, piece],
+            {"tensor": me + 2 * way},
+        )
+
+    def z_forward(k, piece, act):
+        source = [o1, o2, o3][k]
+
+        @pl.when(jnp.logical_and(source < z, z < 3))
+        def _():
+            act(z_copy(k, source * 2 + x, piece, 1))
+
+        @pl.when(jnp.logical_and(source > z, z > 0))
+        def _():
+            act(z_copy(k, source * 2 + x, piece, -1))
+
+    def own_moves(act):
+        for piece in range(PIECES):
+            act(own_copy(piece, 0))
+
+            @pl.when(z < 3)
+            def _():
+                act(own_copy(piece, 1))
+
+            @pl.when(z > 0)
+            def _():
+                act(own_copy(piece, 2))
+
+    own_moves(lambda copy: copy.start())
+
+    def i_copy(shift):
+        to = (me + shift) % 8
+        return remote(
+            inp_ref.at[pl.ds(pl.multiple_of(to * 8, 8), 8)],
+            irecv.at[shift - 1],
+            isem_s.at[shift - 1],
+            isem_r.at[shift - 1],
+            {"tensor": to},
+        )
+
+    for shift in range(1, 8):
+        i_copy(shift).start()
+
+    def stage_copy(which, tile, slot):
+        ref = [gate_ref, up_ref][which]
+        return pltpu.make_async_copy(
+            ref.at[pl.ds(pl.multiple_of(tile * ROWS, ROWS), ROWS)],
+            stage.at[which, slot],
+            stage_sem.at[which, slot],
+        )
+
+    for which in range(2):
+        stage_copy(which, 0, 0).start()
+
+    def multiply(step, first=False):
+        index, piece = steps[step]
+        block = cot_ref if index == 0 else held.at[order[index]]
+        w_copy(step).wait()
+
+        @pl.loop(0, tiles)
+        def _(tile):
+            rows = pl.ds(pl.multiple_of(tile * ROWS, ROWS), ROWS)
+            part = jnp.dot(
+                wbuf[step % W_SLOTS, rows, :],
+                block[pl.ds(piece * depth, depth), :],
+                preferred_element_type=F32,
+            )
+            if first:
+                acc[rows, :] = part
+            else:
+                acc[rows, :] += part
+
+        if step + W_SLOTS < len(steps):
+            w_copy(step + W_SLOTS).start()
+
+    for piece in range(PIECES):
+        multiply(piece, first=piece == 0)
+
+    for tile in range(tiles):
+        slot = tile % 2
+        for which in range(2):
+            if tile + 1 < tiles:
+                stage_copy(which, tile + 1, 1 - slot).start()
+            stage_copy(which, tile, slot).wait()
+
+        @pl.loop(0, ROWS // 64)
+        def _(part):
+            rows = pl.ds(pl.multiple_of(part * 64, 64), 64)
+            target = pl.ds(pl.multiple_of(tile * ROWS + part * 64, 64), 64)
+            activated, slope = silu_parts(stage[0, slot, rows, :].astype(F32))
+            gate_mul[target, :] = stage[1, slot, rows, :].astype(F32) * slope
+            up_mul[target, :] = activated
+
+    for shift in range(1, 8):
+        i_copy(shift).wait_recv()
+    my_rows = pl.ds(pl.multiple_of(me * 8, 8), 8)
+    total = inp_ref[my_rows, :]
+    for shift in range(1, 8):
+        total = total + irecv[shift - 1]
+    iall[core, my_rows, :] = total
+
+    def j_copy(shift):
+        block = iall.at[core, my_rows]
+        return remote(
+            block,
+            block,
+            jsem_s.at[shift - 1],
+            jsem_r.at[shift - 1],
+            {"tensor": (me + shift) % 8},
+        )
+
+    for shift in range(1, 8):
+        j_copy(shift).start()
+
+    for index in range(1, 8):
+        if index == 4:
+            for shift in range(1, 8):
+                j_copy(shift).wait_recv()
+            i_swap = remote(iall.at[core], iall.at[core], dsem.at[0], dsem.at[1], peer)
+            i_swap.start()
+        for piece in range(PIECES):
+            shard = order[index]
+            block = held.at[shard, pl.ds(piece * depth, depth)]
+            remote(
+                block, block, own_send.at[0, piece], recv_sem.at[shard, piece], across
+            ).wait_recv()
+            if index in (1, 3, 5):
+                k = index // 2
+                z_forward(k, piece, lambda copy: copy.start())
+                x_copy(k, shard, piece).start()
+            multiply(index * PIECES + piece)
+
+    rank = pg_ref.shape[1]
+    frows[...] = jnp.zeros_like(frows)
+
+    @pl.loop(0, tiles)
+    def _(tile):
+        rows = pl.ds(pl.multiple_of(tile * ROWS, ROWS), ROWS)
+        grad = acc[rows, :]
+        gate_grad = (grad * gate_mul[rows, :]).astype(BF16)
+        up_grad = (grad * up_mul[rows, :]).astype(BF16)
+        frows[pl.ds(0, rank), :] += contract_first(pg_ref[rows, :], gate_grad)
+        frows[pl.ds(rank, rank), :] += contract_first(pu_ref[rows, :], up_grad)
+
+    def f_copy(shift):
+        to = (me + shift) % 8
+        return remote(
+            frows.at[pl.ds(pl.multiple_of(to * 16, 16), 16)],
+            frecv.at[shift - 1],
+            fsem_s.at[shift - 1],
+            fsem_r.at[shift - 1],
+            {"tensor": to},
+        )
+
+    for shift in range(1, 8):
+        f_copy(shift).start()
+    summed = frows[pl.ds(pl.multiple_of(me * 16, 16), 16), :]
+    for shift in range(1, 8):
+        f_copy(shift).wait_recv()
+        summed = summed + frecv[shift - 1]
+    fall[core] = summed
+    f_swap = remote(fall.at[core], fall.at[core], dsem.at[2], dsem.at[3], peer)
+    f_swap.start()
+    i_swap.wait()
+    f_swap.wait()
+
+    slots = mask_ref.shape[0]
+    for slot in range(slots):
+        value = jnp.zeros((16, rank), F32)
+        for d in range(2):
+            value = value + contract_last(
+                fall[d] * mask_ref[pl.ds(slot, 1), pl.ds(d * toks, toks)], iall[d]
+            )
+        keys[me, pl.ds(slot * 16, 16), :] = value.astype(BF16)
+
+    def k_copy(shift):
+        block = keys.at[me]
+        return remote(
+            block,
+            block,
+            ksem_s.at[shift - 1],
+            ksem_r.at[shift - 1],
+            {"tensor": (me + shift) % 8},
+        )
+
+    for shift in range(1, 8):
+        k_copy(shift).start()
+    for shift in range(1, 8):
+        k_copy(shift).wait_recv()
+    out_ref[...] = keys[...]
+
+    own_moves(lambda copy: copy.wait_send())
+    for k, source in enumerate((o1, o2, o3)):
+        for piece in range(PIECES):
+            z_forward(k, piece, lambda copy: copy.wait_send())
+            x_copy(k, source * 2 + x, piece).wait_send()
+    for shift in range(1, 8):
+        i_copy(shift).wait_send()
+        j_copy(shift).wait_send()
+        f_copy(shift).wait_send()
+        k_copy(shift).wait_send()
+
+
+def fused_keys(cotangent, down_weight, gate_pre, up_pre, proj_gate, proj_up, partial, mask):
+    feats, toks = cotangent.shape
+    hidden, width = down_weight.shape
+    rank = proj_gate.shape[1]
+    slots = mask.shape[0]
+    vmem = pl.BlockSpec(memory_space=pltpu.VMEM)
+    hbm = pl.BlockSpec(memory_space=pl.ANY)
+    sems = pltpu.SemaphoreType.DMA
+    return pl.pallas_call(
+        keys_kernel,
+        out_shape=jax.ShapeDtypeStruct((8, slots * 16, rank), BF16),
+        in_specs=[vmem, hbm, hbm, hbm, vmem, vmem, vmem, vmem],
+        out_specs=vmem,
+        scratch_shapes=[
+            pltpu.VMEM((8, feats, toks), BF16),
+            pltpu.VMEM((W_SLOTS, hidden, feats // PIECES), BF16),
+            pltpu.VMEM((hidden, toks), F32),
+            pltpu.VMEM((hidden, toks), F32),
+            pltpu.VMEM((hidden, toks), F32),
+            pltpu.VMEM((2, 2, ROWS, toks), BF16),
+            pltpu.VMEM((7, 8, toks), F32),
+            pltpu.VMEM((2, rank, toks), F32),
+            pltpu.VMEM((2 * rank, toks), F32),
+            pltpu.VMEM((7, 16, toks), F32),
+            pltpu.VMEM((2, 16, toks), F32),
+            pltpu.VMEM((8, slots * 16, rank), BF16),
+            sems((W_SLOTS,)),
+            sems((2, 2)),
+            sems((8, PIECES)),
+            sems((3, PIECES)),
+            sems((3, PIECES)),
+            sems((3, PIECES)),
+            sems((7,)),
+            sems((7,)),
+            sems((7,)),
+            sems((7,)),
+            sems((7,)),
+            sems((7,)),
+            sems((7,)),
+            sems((7,)),
+            sems((4,)),
+        ],
+        compiler_params=pltpu.CompilerParams(
+            collective_id=0, has_side_effects=True, vmem_limit_bytes=60 * 2**20
+        ),
+        cost_estimate=pl.CostEstimate(
+            flops=2 * hidden * width * toks,
+            bytes_accessed=2 * hidden * (width + 2 * toks),
+            transcendentals=hidden * toks,
+        ),
+    )(cotangent, down_weight, gate_pre, up_pre, proj_gate, proj_up, partial, mask)
+
+
+def per_device_fused(
+    cotangent,
+    layer_input,
+    gate_pre,
+    up_pre,
+    down_weight,
+    proj_input,
+    proj_gate,
+    proj_up,
+    store_slot,
+    example_ids,
+    lengths,
+):
+    toks = cotangent.shape[1]
+    rank = proj_gate.shape[1]
+    seqs = lengths.shape[0]
+    seq_len = toks // seqs
+    core = lax.axis_index("dp")
+    mine = jnp.stack([store_slot, example_ids, lengths])
+    theirs = lax.ppermute(mine, "dp", [(0, 1), (1, 0)])
+    first = jnp.where(core == 0, mine, theirs)
+    second = jnp.where(core == 0, theirs, mine)
+    slot_all, id_all, len_all = jnp.concatenate([first, second], axis=1)
+    wanted = core * seqs + jnp.arange(seqs, dtype=jnp.int32)
+    chosen = slot_all[None, :] == wanted[:, None]
+    position = jnp.arange(seq_len, dtype=jnp.int32)
+    inside = jnp.where(position[None, :] < len_all[:, None], 1.0, 0.0).astype(F32)
+    weight = inside * lax.rsqrt(len_all.astype(F32))[:, None]
+    mask = jnp.where(chosen[:, :, None], weight[None], 0.0).reshape(seqs, 2 * toks)
+    store_ids = jnp.sum(jnp.where(chosen, id_all[None, :], 0), axis=1).astype(jnp.int32)
+    partial = contract_first(proj_input, layer_input)
+    keys = fused_keys(
+        cotangent, down_weight, gate_pre, up_pre, proj_gate, proj_up, partial, mask
+    )
+    keys = keys.reshape(8, seqs, 16, rank).transpose(1, 0, 2, 3)
+    return (keys.reshape(seqs, 2 * rank * rank), store_ids)
+
+
+def per_device_plain(
     cotangent,
     layer_input,
     gate_pre,
@@ -92,8 +522,9 @@
         P(("parts", "dp")),
         P(("parts", "dp")),
     )
+    fits = mesh.shape["tensor"] == 8 and mesh.shape["dp"] == 2
     return jax.shard_map(
-        per_device,
+        per_device_fused if fits else per_device_plain,
         mesh=mesh,
         in_specs=placed,
         out_specs=(P(("parts", "dp"), None), P(("parts", "dp"))),

time: 267 us -> 138 us (0.52)
  waiting for transfers between devices: 194 us -> 0.01 us
  Pallas kernels: 0 us -> 126 us
  matrix products: 47.2 us -> 1.87 us
  between operations: 14.2 us -> 0.7 us
  blocking collectives: 7.48 us -> 0 us
  local copies, waits for them, and re-layouts: 1.4 us -> 6.5 us
    pallas_call x0 -> x1, Pallas kernels: none -> 126 us  [fused_keys(): pl.pallas_call(keys_kernel, out_shape=jax.ShapeDtypeStruct((8, slots * 16...]
    all_gather x1 -> x0, waiting for transfers between devices: 124 us -> none  [per_device(): lax.all_gather(cotangent, 'tensor', axis=0, tiled=True)]
    psum x1 -> x0, waiting for transfers between devices: 69.6 us -> none  [per_device(): summed = lax.psum(partial_rows, 'tensor')]
    dot_general x3 -> x0, matrix products: 40.4 us -> none  [the longest x1 38.8 us: per_device(): jnp.dot(down_weight, lax.all_gather(cotangent, 'tensor', axis=0, tiled=Tr...]
    all_to_all x2 -> x0, blocking collectives: 7.48 us -> none  [the longest x1 3.84 us: per_device(): lax.all_to_all(outgoing, 'dp', split_axis=0, concat_axis=0, tiled=True)]
    dot_general x3 -> x1, matrix products: 6.78 us -> 1.87 us  [contract_first(): lax.dot_general(left, right, (((0,), (0,)), ((), ())), preferred_element_...]
    unnamed x16 -> x13, local copies, waits for them, and re-layouts: 0.05 us -> 4.66 us
  transfers between devices with their start and end apart: 2 -> 1, of which waited for: 2 -> 0; matrix products, arithmetic and copies ran while one was open for 1% -> 5% of each run, Pallas kernels for 0% -> 0%
where the time goes in v1:
time: 138 us; the launch traced here: 137 us
  Pallas kernels  126 us (91%)
  local copies, waits for them, and re-layouts  6.5 us (5%)
  other arithmetic  2.21 us (2%)
  matrix products  1.87 us (1%)
    pallas_call x1, Pallas kernels, fused_keys(): pl.pallas_call(keys_kernel, out_shape=jax.ShapeDtypeStruct((8, slots * 16...  126 us
    unnamed x13, local copies, waits for them, and re-layouts  4.66 us
  transfers between devices with their start and end apart: 1, of which 0 were waited for; matrix products, arithmetic and copies ran while one was open for 5% of the time, Pallas kernels for 0%

profile of v1, /device:TPU:0, one launch (start us, length us, event | category | flops | bytes accessed | tf_op | source)
XLA Modules:
  0.0 137.4 jit_solution(6136026422490801999)
XLA Ops:
  0.6 0.0 copy-start
  0.6 0.0 copy-start.2
  0.7 0.0 copy-start.3
  0.7 0.0 copy-start.4
  0.7 0.8 pad_add_fusion
  1.5 0.5 collective-permute-start
  2.0 2.3 %copy.13.pg_ref = bf16[3584,64]{1,0:T(8,128)(2,1)} copy(bf16[3584,64]{0,1:T(8,128)(2,1)} %param.17) | data formatting | bytes 917504 | tf_op args[6]
  4.2 2.3 %copy.14.pu_ref = bf16[3584,64]{1,0:T(8,128)(2,1)} copy(bf16[3584,64]{0,1:T(8,128)(2,1)} %param.18) | data formatting | bytes 917504 | tf_op args[7]
  6.5 0.0 copy-done
  6.5 1.9 %fusion.inp_ref = f32[64,512]{1,0:T(8,128)} fusion(bf16[1024,64]{0,1:T(8,128)(2,1)} %param.16, bf16[1024,512]{1,0:T(8,128)(2,1)S(1)} %copy-done), kind=kOutput, calls=%fused_computation.15 | convolution fusion | flops 67108864 | bytes 1310720 | tf_op jit(solution)/shard_map/dot_general | solution.py:24
  8.4 0.0 collective-permute-done
  8.4 0.0 copy-done.2
  8.4 0.0 copy-done.3
  8.4 0.0 copy-done.4
  8.4 0.1 pad_add_fusion.1
  8.5 0.7 select_reduce_fusion
  9.2 0.1 broadcast_bitcast_fusion
  9.3 0.1 lt.23
  9.4 0.1 mul.18
  9.4 0.6 bitcast_select_fusion.mask_ref
  10.1 0.0 copy-start.1
  10.1 125.6 %shard_map.122 = bf16[8,64,64]{2,1,0:T(8,128)(2,1)} custom-call(bf16[1024,512]{1,0:T(8,128)(2,1)} %cot_ref.1, bf16[3584,8192]{1,0:T(8,128)(2,1)} %w_ref.1, bf16[3584,512]{1,0:T(8,128)(2,1)} %gate_ref.1, bf16[3584,512]{1,0:T(8,128)(2,1)} %up_ref.1, bf16[3584,64]{1,0:T(8,128)(2,1)} %copy.13.pg_ref, bf16[3584,64]{1,0:T(8,128)(2,1)} %copy.14.pu_ref, ...), custom_call_target="tpu_custom_call" | custom-call | flops 30064771072 | bytes 66060288 | tf_op jit(solution)/shard_map/pallas_call | solution.py:365
  135.7 0.9 copy.15
  136.6 0.8 reshape.86
  137.4 0.0 copy-done.1
  (5 shorter events, 0.0 us)
Async XLA Ops:
  0.6 5.9 %copy-start = (bf16[1024,512]{1,0:T(8,128)(2,1)S(1)}, bf16[1024,512]{1,0:T(8,128)(2,1)}, u32[]{:S(2)}) copy-start(bf16[1024,512]{1,0:T(8,128)(2,1)} %param.12) | copy-start | bytes 3145732
  0.6 7.8 %copy-start.2 = (s32[4]{0:T(128)S(1)}, s32[4]{0:T(128)}, u32[]{:S(2)}) copy-start(s32[4]{0:T(128)} %param.21) | copy-start | bytes 52
  0.7 7.7 %copy-start.3 = (s32[4]{0:T(128)S(1)}, s32[4]{0:T(128)}, u32[]{:S(2)}) copy-start(s32[4]{0:T(128)} %param.20) | copy-start | bytes 52
  0.7 7.7 %copy-start.4 = (s32[4]{0:T(128)S(1)}, s32[4]{0:T(128)}, u32[]{:S(2)}) copy-start(s32[4]{0:T(128)} %param.19) | copy-start | bytes 52
  1.5 6.9 %collective-permute-start = (s32[3,4]{1,0:T(4,128)S(1)}, s32[3,4]{1,0:T(4,128)S(1)}, u32[]{:S(2)}, u32[]{:S(2)}) collective-permute-start(s32[3,4]{1,0:T(4,128)S(1)} %pad_add_fusion), channel_id=1, source_target_pairs={{0,1},{1,0},{2,3},{3,2},{4,5},{5,4},{6,7},{7,6},{8,9},{9,8},{10,11... | collective-permute-start | bytes 152 | tf_op jit(solution)/shard_map/ppermute | solution.py:429
  10.1 127.3 %copy-start.1 = (bf16[1024,512]{1,0:T(8,128)(2,1)S(1)}, bf16[1024,512]{1,0:T(8,128)(2,1)}, u32[]{:S(2)}) copy-start(bf16[1024,512]{1,0:T(8,128)(2,1)} %param.12) | copy-start | bytes 3145732

commit v2 on v1

v2 whole, which is shorter than its diff:
```python
import functools

import jax
import jax.numpy as jnp
from jax import lax
from jax.experimental import pallas as pl
from jax.experimental.pallas import tpu as pltpu
from jax.sharding import PartitionSpec as P

MESH = pl.DeviceIdType.MESH
F32 = jnp.float32
BF16 = jnp.bfloat16
PIECES = 4
PAIRS = 2
W_SLOTS = 3
ROWS = 512
PART = 256


def silu_parts(gate_value):
    sigmoid_gate = jax.nn.sigmoid(gate_value)
    return (gate_value * sigmoid_gate, sigmoid_gate * (1.0 + gate_value * (1.0 - sigmoid_gate)))


def contract_first(left, right):
    return lax.dot_general(
        left, right, (((0,), (0,)), ((), ())), preferred_element_type=jnp.float32
    )


def dot(left, right):
    return jnp.dot(left, right, preferred_element_type=jnp.float32)


def dot_exact(left, right):
    return jnp.dot(
        left, right, precision=lax.Precision.HIGHEST, preferred_element_type=jnp.float32
    )


def contract_last(left, right):
    return lax.dot_general(
        left,
        right,
        (((1,), (1,)), ((), ())),
        precision=lax.Precision.HIGHEST,
        preferred_element_type=jnp.float32,
    )


def keys_kernel(
    mine_ref,
    theirs_ref,
    cot_ref,
    lin_hbm,
    w_ref,
    gate_ref,
    up_ref,
    pi_hbm,
    pg_hbm,
    pu_hbm,
    out_ref,
    perm,
    mask,
    spare,
    packed,
    gate_up_spare,
    lin,
    pi,
    pg,
    pu,
    inp,
    held,
    wbuf,
    acc,
    gate_mul,
    up_mul,
    stage,
    irecv,
    iall,
    ipacked,
    frows,
    frecv,
    fall,
    keys,
    w_sem,
    stage_sem,
    load_sem,
    recv_sem,
    own_send,
    x_send,
    z_send,
    extra_send,
    isem_s,
    isem_r,
    jsem_s,
    jsem_r,
    fsem_s,
    fsem_r,
    ksem_s,
    ksem_r,
    dsem_s,
    dsem_r,
):
    feats, slots_all = cot_ref.shape
    hidden = w_ref.shape[0]
    toks = packed.shape[1]
    seqs = mine_ref.shape[1]
    length = slots_all // seqs
    rank = pg.shape[0]
    depth = feats // PIECES
    wide = feats // PAIRS
    per_pair = PIECES // PAIRS
    tiles = hidden // ROWS
    me = lax.axis_index("tensor")
    core = lax.axis_index("dp")
    z, x = me // 2, me % 2
    other = 1 - x
    o1 = z - 1 + 2 * ((3 - z) // 3)
    o3 = 3 * (1 - z // 2)
    o2 = 6 - z - o1 - o3
    across = {"tensor": z * 2 + other}
    peer = {"dp": 1 - core}

    order = [
        me,
        o1 * 2 + x,
        z * 2 + other,
        o2 * 2 + x,
        o1 * 2 + other,
        o3 * 2 + x,
        o2 * 2 + other,
        o3 * 2 + other,
    ]
    steps = [(shard, pair) for shard in range(8) for pair in range(PAIRS)]

    def w_copy(step):
        index, pair = steps[step]
        start = pl.multiple_of(order[index] * feats + pair * wide, wide)
        return pltpu.make_async_copy(
            w_ref.at[:, pl.ds(start, wide)], wbuf.at[step % W_SLOTS], w_sem.at[step % W_SLOTS]
        )

    loads = [
        pltpu.make_async_copy(source, target, load_sem.at[i])
        for i, (source, target) in enumerate(
            ((lin_hbm, lin), (pi_hbm, pi), (pg_hbm, pg), (pu_hbm, pu))
        )
    ]

    def stage_copy(which, tile):
        ref = [gate_ref, up_ref][which]
        return pltpu.make_async_copy(
            ref.at[pl.ds(tile * ROWS, ROWS)], stage.at[which, tile % 2], stage_sem.at[which, tile % 2]
        )

    loads[0].start()
    loads[1].start()
    for step in range(W_SLOTS):
        w_copy(step).start()
    loads[2].start()
    loads[3].start()
    for which in range(2):
        stage_copy(which, 0).start()

    barrier = pltpu.get_barrier_semaphore()
    for shift in range(1, 8):
        pl.semaphore_signal(
            barrier, inc=1, device_id={"tensor": (me + shift) % 8}, device_id_type=MESH
        )
    pl.semaphore_signal(barrier, inc=1, device_id=peer, device_id_type=MESH)

    def remote(src, dst, send, recv, where):
        return pltpu.make_async_remote_copy(
            src_ref=src,
            dst_ref=dst,
            send_sem=send,
            recv_sem=recv,
            device_id=where,
            device_id_type=MESH,
        )

    def lengths_of(ref):
        return [ref[2, s] for s in range(seqs)]

    def plan(ref):
        long = lengths_of(ref)
        count = sum(long[1:], long[0])
        spill = jnp.maximum(count - toks, 0)
        kept = long[:-1] + [long[-1] - spill]
        starts = [jnp.int32(0)]
        for value in long[:-1]:
            starts.append(starts[-1] + value)
        return long, count, spill, kept, starts

    def make_perm(view, own, far):
        long, count, spill, kept, starts = plan(own)
        far_long, _, far_spill, far_kept, _ = plan(far)
        row = lax.broadcasted_iota(jnp.int32, (length, toks), 0)
        gap = lax.broadcasted_iota(jnp.int32, (length, toks), 1) - row
        for s in range(seqs):
            hit = jnp.logical_and(gap == starts[s], row < kept[s])
            perm[view, pl.ds(s * length, length), :] = jnp.where(hit, 1.0, 0.0).astype(BF16)
        hit = jnp.logical_and(
            gap == count - far_kept[-1],
            jnp.logical_and(row >= far_kept[-1], row < far_long[-1]),
        )
        perm[view, pl.ds(slots_all, length), :] = jnp.where(hit, 1.0, 0.0).astype(BF16)

    def make_mask(view, own, far):
        long, count, spill, kept, starts = plan(own)
        far_long, _, far_spill, _, _ = plan(far)
        column = lax.broadcasted_iota(jnp.int32, (seqs, toks), 1)
        wanted = lax.broadcasted_iota(jnp.int32, (seqs, toks), 0) + core * seqs
        entries = [
            (starts[s], kept[s], long[s], own[0, s]) for s in range(seqs)
        ] + [(count, far_spill, far_long[-1], far[0, seqs - 1])]
        value = jnp.zeros((seqs, toks), F32)
        for first, many, full, slot in entries:
            hit = jnp.logical_and(column >= first, column < first + many)
            hit = jnp.logical_and(hit, wanted == slot)
            scale = lax.rsqrt(jnp.full((seqs, toks), full, jnp.int32).astype(F32))
            value = value + jnp.where(hit, scale, 0.0)
        mask[view] = value

    last = pl.ds(slots_all - length, length)
    make_perm(0, mine_ref, theirs_ref)
    pl.semaphore_wait(barrier, 8)

    c_swap = remote(cot_ref.at[:, last], spare, dsem_s.at[0], dsem_r.at[0], peer)
    c_swap.start()
    g_swaps = [
        remote(ref.at[:, last], gate_up_spare.at[i], dsem_s.at[1 + i], dsem_r.at[1 + i], peer)
        for i, ref in enumerate((gate_ref, up_ref))
    ]

    def own_copy(piece, way):
        where = [
            across,
            {"tensor": jnp.minimum(me + 2, 6 + x)},
            {"tensor": jnp.maximum(me - 2, x)},
        ][way]
        return remote(
            packed.at[pl.ds(piece * depth, depth)],
            held.at[me, pl.ds(piece * depth, depth)],
            own_send.at[way, piece],
            recv_sem.at[me, piece],
            where,
        )

    def block_copy(shard, piece, send, where):
        block = held.at[shard, pl.ds(piece * depth, depth)]
        return remote(block, block, send, recv_sem.at[shard, piece], where)

    def x_copy(k, shard, piece):
        return block_copy(shard, piece, x_send.at[k, piece], across)

    def z_forward(k, piece, act):
        source = [o1, o2, o3][k]
        for way, holds in (
            (1, jnp.logical_and(source < z, z < 3)),
            (-1, jnp.logical_and(source > z, z > 0)),
        ):

            @pl.when(holds)
            def _():
                act(
                    block_copy(
                        source * 2 + x, piece, z_send.at[k, piece], {"tensor": me + 2 * way}
                    )
                )

    def extra_forward(piece, act):
        for i, (way, holds) in enumerate(((1, z < 3), (-1, z == 1))):

            @pl.when(holds)
            def _():
                act(
                    block_copy(
                        z * 2 + other, piece, extra_send.at[i, piece], {"tensor": me + 2 * way}
                    )
                )

    def own_moves(piece, act):
        act(own_copy(piece, 0))

        @pl.when(z < 3)
        def _():
            act(own_copy(piece, 1))

        @pl.when(z > 0)
        def _():
            act(own_copy(piece, 2))

    def start(copy):
        copy.start()

    def wait_send(copy):
        copy.wait_send()

    c_swap.wait_recv()
    for piece in range(PIECES):
        rows = pl.ds(piece * depth, depth)
        packed[rows, :] = (
            dot(cot_ref[rows, :], perm[0, pl.ds(0, slots_all), :])
            + dot(spare[rows, :], perm[0, pl.ds(slots_all, length), :])
        ).astype(BF16)
        own_moves(piece, start)
    for swap in g_swaps:
        swap.start()

    loads[0].wait()
    loads[1].wait()
    inp[...] = dot(pi[...], lin[...])

    def i_copy(shift):
        to = (me + shift) % 8
        return remote(
            inp.at[pl.ds(pl.multiple_of(to * 8, 8), 8)],
            irecv.at[shift - 1],
            isem_s.at[shift - 1],
            isem_r.at[shift - 1],
            {"tensor": to},
        )

    for shift in range(1, 8):
        i_copy(shift).start()

    def multiply(step, first=False):
        index, pair = steps[step]
        block = packed if index == 0 else held.at[order[index]]
        w_copy(step).wait()

        @pl.loop(0, tiles)
        def _(tile):
            rows = pl.ds(pl.multiple_of(tile * ROWS, ROWS), ROWS)
            part = dot(wbuf[step % W_SLOTS, rows, :], block[pl.ds(pair * wide, wide), :])
            if first:
                acc[rows, :] = part
            else:
                acc[rows, :] += part

        if step + W_SLOTS < len(steps):
            w_copy(step + W_SLOTS).start()

    def slopes(tile):
        slot = tile % 2
        for which in range(2):
            if tile + 1 < tiles:
                stage_copy(which, tile + 1).start()
            stage_copy(which, tile).wait()

        @pl.loop(0, ROWS // PART)
        def _(part):
            rows = pl.ds(pl.multiple_of(part * PART, PART), PART)
            target = pl.ds(pl.multiple_of(tile * ROWS + part * PART, PART), PART)
            gate_value, up_value = [
                dot(stage[which, slot, rows, :], perm[0, pl.ds(0, slots_all), :])
                + dot(gate_up_spare[which, target, :], perm[0, pl.ds(slots_all, length), :])
                for which in range(2)
            ]
            activated, slope = silu_parts(gate_value)
            gate_mul[target, :] = up_value * slope
            up_mul[target, :] = activated

    for pair in range(PAIRS):
        multiply(pair, first=pair == 0)
    for swap in g_swaps:
        swap.wait_recv()
    for tile in range(3):
        slopes(tile)

    my_rows = pl.ds(pl.multiple_of(me * 8, 8), 8)

    def j_copy(shift):
        block = iall.at[core, my_rows]
        return remote(
            block,
            block,
            jsem_s.at[shift - 1],
            jsem_r.at[shift - 1],
            {"tensor": (me + shift) % 8},
        )

    for index in range(1, 8):
        if index == 3:
            for shift in range(1, 8):
                i_copy(shift).wait_recv()
            total = inp[my_rows, :]
            for shift in range(1, 8):
                total = total + irecv[shift - 1]
            iall[core, my_rows, :] = total
            for shift in range(1, 8):
                j_copy(shift).start()
            make_perm(1, theirs_ref, mine_ref)
            make_mask(0, mine_ref, theirs_ref)
            make_mask(1, theirs_ref, mine_ref)
        if index == 4:
            for shift in range(1, 8):
                j_copy(shift).wait_recv()
            i_swap = remote(iall.at[core], iall.at[core], dsem_s.at[3], dsem_r.at[3], peer)
            i_swap.start()
        if index == 6:
            i_swap.wait_recv()
            for view, near in ((0, core), (1, 1 - core)):
                ipacked[view] = dot_exact(
                    iall[near], perm[view, pl.ds(0, slots_all), :].astype(F32)
                ) + dot_exact(
                    iall[1 - near, :, pl.ds(slots_all - length, length)],
                    perm[view, pl.ds(slots_all, length), :].astype(F32),
                )
        shard = order[index]
        for pair in range(PAIRS):
            for piece in range(pair * per_pair, (pair + 1) * per_pair):
                block_copy(shard, piece, own_send.at[0, piece], across).wait_recv()
                if index in (1, 3, 5):
                    k = index // 2
                    z_forward(k, piece, start)
                    if k > 0 or piece < PIECES // 2:
                        x_copy(k, shard, piece).start()
                if index == 2 and piece >= PIECES // 2:
                    extra_forward(piece, start)
            multiply(index * PAIRS + pair)
        if index <= 2:
            slopes(1 + 2 * index)
            slopes(2 + 2 * index)

    loads[2].wait()
    loads[3].wait()
    gate_sum = jnp.zeros((rank, toks), F32)
    up_sum = jnp.zeros((rank, toks), F32)
    for tile in range(tiles):
        rows = pl.ds(tile * ROWS, ROWS)
        grad = acc[rows, :]
        gate_grad = (grad * gate_mul[rows, :]).astype(BF16)
        up_grad = (grad * up_mul[rows, :]).astype(BF16)
        gate_sum = gate_sum + dot(pg[:, rows], gate_grad)
        up_sum = up_sum + dot(pu[:, rows], up_grad)
    frows[pl.ds(0, rank), :] = gate_sum
    frows[pl.ds(rank, rank), :] = up_sum

    def f_copy(shift):
        to = (me + shift) % 8
        return remote(
            frows.at[pl.ds(pl.multiple_of(to * 16, 16), 16)],
            frecv.at[shift - 1],
            fsem_s.at[shift - 1],
            fsem_r.at[shift - 1],
            {"tensor": to},
        )

    for shift in range(1, 8):
        f_copy(shift).start()
    summed = frows[pl.ds(pl.multiple_of(me * 16, 16), 16), :]
    for shift in range(1, 8):
        f_copy(shift).wait_recv()
        summed = summed + frecv[shift - 1]
    fall[core] = summed
    f_swap = remote(fall.at[core], fall.at[core], dsem_s.at[4], dsem_r.at[4], peer)
    f_swap.start()
    f_swap.wait_recv()

    for s in range(seqs):
        value = jnp.zeros((16, rank), F32)
        for view, near in ((0, core), (1, 1 - core)):
            value = value + contract_last(
                fall[near] * mask[view, pl.ds(s, 1), :], ipacked[view]
            )
        keys[me, pl.ds(s * 16, 16), :] = value.astype(BF16)

    def k_copy(shift):
        block = keys.at[me]
        return remote(
            block,
            block,
            ksem_s.at[shift - 1],
            ksem_r.at[shift - 1],
            {"tensor": (me + shift) % 8},
        )

    for shift in range(1, 8):
        k_copy(shift).start()

    for swap in [c_swap, i_swap, f_swap] + g_swaps:
        swap.wait_send()
    for piece in range(PIECES):
        own_moves(piece, wait_send)
        if piece >= PIECES // 2:
            extra_forward(piece, wait_send)
        for k, source in enumerate((o1, o2, o3)):
            z_forward(k, piece, wait_send)
            if k > 0 or piece < PIECES // 2:
                x_copy(k, source * 2 + x, piece).wait_send()
    for shift in range(1, 8):
        i_copy(shift).wait_send()
        j_copy(shift).wait_send()
        f_copy(shift).wait_send()

    for shift in range(1, 8):
        k_copy(shift).wait_recv()
    for t in range(8):
        for s in range(seqs):
            out_ref[s, pl.ds(t * 16, 16), :] = keys[t, pl.ds(s * 16, 16), :]
    for shift in range(1, 8):
        k_copy(shift).wait_send()


def fused_keys(mine, theirs, cotangent, layer_input, down_weight, gate_pre, up_pre, pi, pg, pu):
    feats, slots_all = cotangent.shape
    hidden, width = down_weight.shape
    rank = pg.shape[0]
    seqs = mine.shape[1]
    length = slots_all // seqs
    toks = slots_all - length
    smem = pl.BlockSpec(memory_space=pltpu.SMEM)
    vmem = pl.BlockSpec(memory_space=pltpu.VMEM)
    hbm = pl.BlockSpec(memory_space=pl.ANY)
    sems = pltpu.SemaphoreType.DMA
    return pl.pallas_call(
        keys_kernel,
        out_shape=jax.ShapeDtypeStruct((seqs, 2 * rank, rank), BF16),
        in_specs=[smem, smem, vmem] + [hbm] * 7,
        out_specs=vmem,
        scratch_shapes=[
            pltpu.VMEM((2, slots_all + length, toks), BF16),
            pltpu.VMEM((2, seqs, toks), F32),
            pltpu.VMEM((feats, length), BF16),
            pltpu.VMEM((feats, toks), BF16),
            pltpu.VMEM((2, hidden, length), BF16),
            pltpu.VMEM((feats, slots_all), BF16),
            pltpu.VMEM((rank, feats), BF16),
            pltpu.VMEM((rank, hidden), BF16),
            pltpu.VMEM((rank, hidden), BF16),
            pltpu.VMEM((rank, slots_all), F32),
            pltpu.VMEM((8, feats, toks), BF16),
            pltpu.VMEM((W_SLOTS, hidden, feats // PAIRS), BF16),
            pltpu.VMEM((hidden, toks), F32),
            pltpu.VMEM((hidden, toks), F32),
            pltpu.VMEM((hidden, toks), F32),
            pltpu.VMEM((2, 2, ROWS, slots_all), BF16),
            pltpu.VMEM((7, 8, slots_all), F32),
            pltpu.VMEM((2, rank, slots_all), F32),
            pltpu.VMEM((2, rank, toks), F32),
            pltpu.VMEM((2 * rank, toks), F32),
            pltpu.VMEM((7, 16, toks), F32),
            pltpu.VMEM((2, 16, toks), F32),
            pltpu.VMEM((8, seqs * 16, rank), BF16),
            sems((W_SLOTS,)),
            sems((2, 2)),
            sems((4,)),
            sems((8, PIECES)),
            sems((3, PIECES)),
            sems((3, PIECES)),
            sems((3, PIECES)),
            sems((2, PIECES)),
        ]
        + [sems((7,))] * 8
        + [sems((5,))] * 2,
        compiler_params=pltpu.CompilerParams(
            collective_id=0, has_side_effects=True, vmem_limit_bytes=60 * 2**20
        ),
        cost_estimate=pl.CostEstimate(
            flops=2 * hidden * width * toks,
            bytes_accessed=2 * hidden * (width + 2 * slots_all),
            transcendentals=hidden * toks,
        ),
    )(mine, theirs, cotangent, layer_input, down_weight, gate_pre, up_pre, pi, pg, pu)


def per_device_fused(
    cotangent,
    layer_input,
    gate_pre,
    up_pre,
    down_weight,
    proj_input,
    proj_gate,
    proj_up,
    store_slot,
    example_ids,
    lengths,
):
    rank = proj_gate.shape[1]
    seqs = lengths.shape[0]
    core = lax.axis_index("dp")
    mine = jnp.stack([store_slot, example_ids, lengths])
    theirs = lax.ppermute(mine, "dp", [(0, 1), (1, 0)])
    wanted = core * seqs + jnp.arange(seqs, dtype=jnp.int32)
    both = jnp.concatenate([mine, theirs], axis=1)
    chosen = both[0][None, :] == wanted[:, None]
    store_ids = jnp.sum(jnp.where(chosen, both[1][None, :], 0), axis=1).astype(jnp.int32)
    keys = fused_keys(
        mine,
        theirs,
        cotangent,
        layer_input,
        down_weight,
        gate_pre,
        up_pre,
        proj_input.T,
        proj_gate.T,
        proj_up.T,
    )
    return (keys.reshape(seqs, 2 * rank * rank), store_ids)


def per_device_plain(
    cotangent,
    layer_input,
    gate_pre,
    up_pre,
    down_weight,
    proj_input,
    proj_gate,
    proj_up,
    store_slot,
    example_ids,
    lengths,
):
    tok_count = cotangent.shape[1]
    proj_rank = proj_gate.shape[1]
    seq_count = lengths.shape[0]
    seq_len = tok_count // seq_count
    hidden_grad = jnp.dot(
        down_weight,
        lax.all_gather(cotangent, "tensor", axis=0, tiled=True),
        preferred_element_type=jnp.float32,
    )
    input_partial = contract_first(proj_input, layer_input)
    gate_value = gate_pre.astype(jnp.float32)
    up_value = up_pre.astype(jnp.float32)
    activated, slope = silu_parts(gate_value)
    gate_grad = (hidden_grad * up_value * slope).astype(jnp.bfloat16)
    up_grad = (hidden_grad * activated).astype(jnp.bfloat16)
    gate_factor = contract_first(proj_gate, gate_grad)
    up_factor = contract_first(proj_up, up_grad)
    partial_rows = jnp.concatenate([gate_factor, up_factor, input_partial], axis=0)
    inverse_root = lax.rsqrt(lengths.astype(jnp.float32))
    summed = lax.psum(partial_rows, "tensor")
    input_factor = summed[2 * proj_rank :]
    position = jnp.arange(seq_len, dtype=jnp.int32)
    inside = jnp.where(position[None, :] < lengths[:, None], 1.0, 0.0).astype(jnp.float32)
    weight = inside * inverse_root[:, None]
    grads_three = summed[: 2 * proj_rank].reshape(2, proj_rank, seq_count, seq_len)
    inputs_three = input_factor.reshape(proj_rank, seq_count, seq_len)
    key_values = jnp.einsum(
        "gael,bel,el->egab", grads_three, inputs_three, weight, precision=lax.Precision.HIGHEST
    )
    key_values = key_values.reshape(seq_count, -1)
    key_rows = key_values.astype(jnp.bfloat16)
    dp_count = lax.axis_size("dp")
    slot_index = jnp.arange(dp_count * seq_count, dtype=jnp.int32)
    chosen = store_slot[None, :] == slot_index[:, None]
    outgoing = jnp.dot(
        chosen.astype(jnp.bfloat16), key_rows, preferred_element_type=jnp.float32
    ).astype(jnp.bfloat16)
    outgoing = outgoing.reshape(dp_count, seq_count, -1)
    outgoing_ids = jnp.sum(jnp.where(chosen, example_ids[None, :], 0), axis=1).reshape(
        dp_count, seq_count
    )
    arrived, arrived_ids = (
        lax.all_to_all(outgoing, "dp", split_axis=0, concat_axis=0, tiled=True),
        lax.all_to_all(outgoing_ids, "dp", split_axis=0, concat_axis=0, tiled=True),
    )
    store_keys = jnp.sum(arrived.astype(jnp.float32), axis=0).astype(jnp.bfloat16)
    store_ids = jnp.sum(arrived_ids, axis=0).astype(jnp.int32)
    return (store_keys, store_ids)


def solution(mesh):
    placed = (
        P("tensor", ("parts", "dp")),
        P("tensor", ("parts", "dp")),
        P("tensor", ("parts", "dp")),
        P("tensor", ("parts", "dp")),
        P("tensor", None),
        P("tensor", None),
        P("tensor", None),
        P("tensor", None),
        P(("parts", "dp")),
        P(("parts", "dp")),
        P(("parts", "dp")),
    )
    fits = mesh.shape["tensor"] == 8 and mesh.shape["dp"] == 2
    return jax.shard_map(
        per_device_fused if fits else per_device_plain,
        mesh=mesh,
        in_specs=placed,
        out_specs=(P(("parts", "dp"), None), P(("parts", "dp"))),
        check_vma=False,
    )
```

time: 138 us -> 120 us (0.87)
  Pallas kernels: 126 us -> 114 us
  local copies, waits for them, and re-layouts: 6.5 us -> 1.69 us
  matrix products: 1.87 us -> 0 us
    pallas_call x1, Pallas kernels: 126 us -> 114 us  [fused_keys(): pl.pallas_call(keys_kernel, out_shape=jax.ShapeDtypeStruct((seqs, 2 * ran...]
    unnamed x13 -> x4, local copies, waits for them, and re-layouts: 4.66 us -> 0.01 us
    dot_general x1 -> x0, matrix products: 1.87 us -> none  [contract_first(): lax.dot_general(left, right, (((0,), (0,)), ((), ())), preferred_element_...]
  transfers between devices with their start and end apart: 1 -> 1, of which waited for: 0 -> 1; matrix products, arithmetic and copies ran while one was open for 5% -> 0% of each run, Pallas kernels for 0% -> 0%
where the time goes in v2:
time: 120 us
  Pallas kernels  114 us (95%)
  other arithmetic  2.16 us (2%)
  local copies, waits for them, and re-layouts  1.69 us (1%)
    pallas_call x1, Pallas kernels, fused_keys(): pl.pallas_call(keys_kernel, out_shape=jax.ShapeDtypeStruct((seqs, 2 * ran...  114 us
  transfers between devices with their start and end apart: 1, of which 1 were waited for; matrix products, arithmetic and copies ran while one was open for 0% of the time, Pallas kernels for 0%

profile of v2, /device:TPU:0, one launch (start us, length us, event | category | flops | bytes accessed | tf_op | source)
XLA Modules:
  0.0 119.9 jit_solution(218646365546045634)
XLA Ops:
  0.6 0.7 pad_add_fusion.mine_ref
  1.3 0.0 copy-start
  1.3 0.5 collective-permute-start
  1.9 0.8 collective-permute-done.theirs_ref
  2.7 0.0 copy-start.1
  2.7 0.8 pad_add_fusion.1
  3.4 0.0 copy-done
  3.4 0.0 copy-done.1
  3.4 114.0 %shard_map.122 = bf16[4,128,64]{2,1,0:T(8,128)(2,1)} custom-call(s32[3,4]{1,0:T(4,128)} %copy-done, s32[3,4]{1,0:T(4,128)} %copy-done.1, bf16[1024,512]{1,0:T(8,128)(2,1)} %cot_ref.1, bf16[1024,512]{1,0:T(8,128)(2,1)} %lin_hbm.1, bf16[3584,8192]{1,0:T(8,128)(2,1)} %w_ref.1, bf16[3584,512]{1,0:T(8,128)(2,1)} %gate_ref.1, bf16[3584,512]{1,0:T(8,128)(2,1)} %up_ref.1, ...), custom_call_target="tpu_custom_call" | custom-call | flops 22548578304 | bytes 66060288 | tf_op jit(solution)/shard_map/pallas_call | solution.py:519
  117.5 1.7 %reshape.11 = bf16[4,8192]{1,0:T(4,128)(2,1)} reshape(bf16[4,128,64]{2,1,0:T(8,128)(2,1)} %shard_map.122) | data formatting | bytes 131072 | tf_op jit(solution)/shard_map/reshape | solution.py:604
  119.2 0.7 select_reduce_fusion
  (2 shorter events, 0.0 us)
Async XLA Ops:
  1.3 2.1 %copy-start = (s32[3,4]{1,0:T(4,128)}, s32[3,4]{1,0:T(4,128)S(1)}, u32[]{:S(2)}) copy-start(s32[3,4]{1,0:T(4,128)S(1)} %pad_add_fusion.mine_ref) | copy-start | bytes 148
  1.3 1.3 %collective-permute-start = (s32[3,4]{1,0:T(4,128)S(1)}, s32[3,4]{1,0:T(4,128)S(1)}, u32[]{:S(2)}, u32[]{:S(2)}) collective-permute-start(s32[3,4]{1,0:T(4,128)S(1)} %pad_add_fusion.mine_ref), channel_id=1, source_target_pairs={{0,1},{1,0},{2,3},{3,2},{4,5},{5,4},{6,7},{7,6},{8,9},{9,8},{10,11... | collective-permute-start | bytes 152 | tf_op jit(solution)/shard_map/ppermute | solution.py:587
  2.7 0.8 copy-start.1

commit v3 on v2

--- a/solution.py
+++ b/solution.py
@@ -331,9 +331,9 @@
         block = packed if index == 0 else held.at[order[index]]
         w_copy(step).wait()
 
-        @pl.loop(0, tiles)
+        @pl.loop(0, 2)
         def _(tile):
-            rows = pl.ds(pl.multiple_of(tile * ROWS, ROWS), ROWS)
+            rows = pl.ds(pl.multiple_of(tile * (hidden // 2), 256), hidden // 2)
             part = dot(wbuf[step % W_SLOTS, rows, :], block[pl.ds(pair * wide, wide), :])
             if first:
                 acc[rows, :] = part

time: 120 us -> 115 us (0.958)
  Pallas kernels: 114 us -> 108 us
    pallas_call x1, Pallas kernels: 114 us -> 108 us  [fused_keys(): pl.pallas_call(keys_kernel, out_shape=jax.ShapeDtypeStruct((seqs, 2 * ran...]
where the time goes in v3:
time: 115 us; the launch traced here: 114 us
  Pallas kernels  108 us (94%)
  other arithmetic  2.16 us (2%)
  local copies, waits for them, and re-layouts  1.69 us (1%)
    pallas_call x1, Pallas kernels, fused_keys(): pl.pallas_call(keys_kernel, out_shape=jax.ShapeDtypeStruct((seqs, 2 * ran...  108 us
  transfers between devices with their start and end apart: 1, of which 1 were waited for; matrix products, arithmetic and copies ran while one was open for 0% of the time, Pallas kernels for 0%

profile of v3, /device:TPU:0, one launch (start us, length us, event | category | flops | bytes accessed | tf_op | source)
XLA Modules:
  0.0 114.3 jit_solution(12093903660408793233)
XLA Ops:
  0.6 0.7 pad_add_fusion.mine_ref
  1.3 0.0 copy-start
  1.3 0.5 collective-permute-start
  1.9 0.8 collective-permute-done.theirs_ref
  2.7 0.0 copy-start.1
  2.7 0.8 pad_add_fusion.1
  3.4 0.0 copy-done
  3.4 0.0 copy-done.1
  3.4 108.5 %shard_map.122 = bf16[4,128,64]{2,1,0:T(8,128)(2,1)} custom-call(s32[3,4]{1,0:T(4,128)} %copy-done, s32[3,4]{1,0:T(4,128)} %copy-done.1, bf16[1024,512]{1,0:T(8,128)(2,1)} %cot_ref.1, bf16[1024,512]{1,0:T(8,128)(2,1)} %lin_hbm.1, bf16[3584,8192]{1,0:T(8,128)(2,1)} %w_ref.1, bf16[3584,512]{1,0:T(8,128)(2,1)} %gate_ref.1, bf16[3584,512]{1,0:T(8,128)(2,1)} %up_ref.1, ...), custom_call_target="tpu_custom_call" | custom-call | flops 22548578304 | bytes 66060288 | tf_op jit(solution)/shard_map/pallas_call | solution.py:519
  111.9 1.7 %reshape.11 = bf16[4,8192]{1,0:T(4,128)(2,1)} reshape(bf16[4,128,64]{2,1,0:T(8,128)(2,1)} %shard_map.122) | data formatting | bytes 131072 | tf_op jit(solution)/shard_map/reshape | solution.py:604
  113.6 0.7 select_reduce_fusion
  (2 shorter events, 0.0 us)
Async XLA Ops:
  1.3 2.1 %copy-start = (s32[3,4]{1,0:T(4,128)}, s32[3,4]{1,0:T(4,128)S(1)}, u32[]{:S(2)}) copy-start(s32[3,4]{1,0:T(4,128)S(1)} %pad_add_fusion.mine_ref) | copy-start | bytes 148
  1.3 1.3 %collective-permute-start = (s32[3,4]{1,0:T(4,128)S(1)}, s32[3,4]{1,0:T(4,128)S(1)}, u32[]{:S(2)}, u32[]{:S(2)}) collective-permute-start(s32[3,4]{1,0:T(4,128)S(1)} %pad_add_fusion.mine_ref), channel_id=1, source_target_pairs={{0,1},{1,0},{2,3},{3,2},{4,5},{5,4},{6,7},{7,6},{8,9},{9,8},{10,11... | collective-permute-start | bytes 152 | tf_op jit(solution)/shard_map/ppermute | solution.py:587
  2.7 0.8 copy-start.1
